TPU v7x, 512 devices: a whole 4x8x8 slice. The times are simulated.
512 devices in a mesh: queue: 32 (over x, z_hi, core), seq: 16 (over y, z_lo).
Axes of the slice: x: 4, y: 8, z: 8 (z_hi: 4, z_lo: 2; z = z_hi * 2 + z_lo), core: 2. Of those that a mesh axis runs over, the one named last changes fastest.
Arguments:
- query_rows: bfloat16 [32, 2048, 4096], P('queue', 'seq'), may hold values from -140 to 140
- key_rows: bfloat16 [32, 2048, 4096], P('queue', 'seq'), may hold values from -6 to 6
- value_rows: bfloat16 [32, 2048, 4096], P('queue', 'seq'), may hold values from -6 to 6
- level_gains: float32 [50, 4096], replicated, may hold values from 0.1 to 1.9
- noise_levels: int32 [32], P('queue'), may hold values from 0 to 49
- halo_frames: int32 [32], P('queue'), may hold values from 1 to 4, as said below
Outputs:
- advanced: bfloat16 [32, 2048, 4096], P('queue', 'seq')
Inputs may be any that keep to these rules, and one draw needn't show every extreme that they name: `halo_frames`: both 1 and 4 are taken by some group other than group 0.
All inputs are finite; a program needn't handle non-finite values.
Results may differ from a plain program's by a relative error of at most 0.0049.
Values may be sent and summed in bfloat16 or wider, within the bound.
A program may use at most 64 MiB of HBM per device.

v0:
```python
import jax
import jax.numpy as jnp
from jax import lax
from jax.sharding import PartitionSpec as P

HEADS_DEV = 2
HD = 128
FTOK = 128
HALO = 4
LEVELS = 50


def passed_along(value, axis, steps):
    count = lax.axis_size(axis)
    first, last = (max(0, -steps), min(count, count - steps))
    return lax.ppermute(value, axis, [(source, source + steps) for source in range(first, last)])


def shifted(value, axis, steps):
    count = lax.axis_size(axis)
    pairs = [(source, (source + steps) % count) for source in range(count)]
    return lax.ppermute(value, axis, pairs)


def edge_shift(key_side, value_side):
    edge_width = HALO * FTOK
    group_tokens = key_side.shape[1]
    edge_keys = key_side[:, group_tokens - edge_width :]
    edge_values = value_side[:, group_tokens - edge_width :]
    return passed_along((edge_keys, edge_values), "queue", 1)


def back_exchange(normed):
    return lax.all_to_all(normed, "seq", split_axis=1, concat_axis=2, tiled=True)


def per_device(query_rows, key_rows, value_rows, level_gains, noise_levels, halo_frames):
    query_heads, key_heads, value_heads = (
        lax.all_to_all(query_rows, "seq", split_axis=2, concat_axis=1, tiled=True),
        lax.all_to_all(key_rows, "seq", split_axis=2, concat_axis=1, tiled=True),
        lax.all_to_all(value_rows, "seq", split_axis=2, concat_axis=1, tiled=True),
    )
    edge_keys, edge_values = edge_shift(key_heads, value_heads)
    group_tokens = query_heads.shape[1]
    head_width = HEADS_DEV * HD
    edge_width = HALO * FTOK
    onehot = (jnp.arange(LEVELS, dtype=jnp.int32) == noise_levels[0]).astype(jnp.float32)
    full_gain = jnp.dot(onehot, level_gains, precision=lax.Precision.HIGHEST)
    gain_slice = lax.dynamic_slice_in_dim(full_gain, lax.axis_index("seq") * head_width, head_width)
    head_gains = gain_slice.reshape(HEADS_DEV, HD)
    positions = jnp.arange(edge_width, dtype=jnp.int32)
    edge_visible = (positions >= (HALO - halo_frames[0]) * FTOK) & (lax.axis_index("queue") > 0)
    mask_all = jnp.concatenate([edge_visible, jnp.ones((group_tokens,), dtype=bool)], axis=0)
    all_keys = jnp.concatenate([edge_keys[0], key_heads[0]], axis=0).reshape(-1, HEADS_DEV, HD)
    all_values = jnp.concatenate([edge_values[0], value_heads[0]], axis=0).reshape(
        -1, HEADS_DEV, HD
    )
    score_scale = HD ** (-0.5)
    block_rows = min(512, group_tokens)
    query_blocks = query_heads[0].reshape(group_tokens // block_rows, block_rows, HEADS_DEV, HD)

    def attend_block(query_block):
        scores = (
            jnp.einsum("qhd,khd->hqk", query_block, all_keys, preferred_element_type=jnp.float32)
            * score_scale
        )
        scores = jnp.where(mask_all[None, None, :], scores, jnp.float32(-1e30))
        top_score = jnp.max(scores, axis=-1, keepdims=True)
        expon = jnp.exp(scores - top_score)
        weights = (expon / jnp.sum(expon, axis=-1, keepdims=True)).astype(jnp.bfloat16)
        mixed = jnp.einsum("hqk,khd->qhd", weights, all_values, preferred_element_type=jnp.float32)
        mean_sq = jnp.mean(mixed * mixed, axis=-1, keepdims=True)
        normed_block = mixed * lax.rsqrt(mean_sq + 1e-06) * head_gains[None, :, :]
        return normed_block.astype(jnp.bfloat16).reshape(block_rows, head_width)

    normed = lax.map(attend_block, query_blocks).reshape(1, group_tokens, head_width)
    token_layout = back_exchange(normed)
    return shifted(token_layout, "queue", 1)


def solution(mesh):
    placed = (
        P("queue", "seq", None),
        P("queue", "seq", None),
        P("queue", "seq", None),
        P(),
        P("queue"),
        P("queue"),
    )
    return jax.shard_map(
        per_device, mesh=mesh, in_specs=placed, out_specs=P("queue", "seq", None), check_vma=False
    )
```

profile of v0, /device:TPU:56, one launch (start us, length us, event | category | flops | bytes accessed | tf_op | source)
XLA Modules:
  0.0 320.7 jit_solution(10110900823617557730)
XLA Ops:
  0.0 5.1 %copy.57 = bf16[1,128,4096]{1,0,2:T(2,128)(2,1)S(1)} copy(bf16[1,128,4096]{2,1,0:T(8,128)(2,1)} %param.9) | data formatting | bytes 2097152 | tf_op args[1]
  5.7 23.3 %reduce.1 = bf16[4096,128]{1,0:T(8,128)(2,1)} reduce(bf16[4096,1,128]{2,1,0:T(2,128)(2,1)S(1)} %bitcast.83, bf16[]{:T(256)} %broadcast.40), dimensions={1}, to_apply=%bitcast.45.reduce_sub_computation | reduce | bytes 2097154
  31.2 9.3 %all-to-all-start.1 = ((bf16[16,2,16384]{2,1,0:T(2,128)(2,1)}), bf16[16,2,16384]{2,1,0:T(2,128)(2,1)}, u32[]{:S(2)}, u32[]{:S(2)}) async-start(bf16[16,2,16384]{2,1,0:T(2,128)(2,1)} %reshape.39), calls=%async_computation.1 | async-start | bytes 2097152 | tf_op jit(solution)/shard_map/all_to_all | solution.py:40
  40.5 5.0 %copy.61 = bf16[1,128,4096]{1,0,2:T(2,128)(2,1)S(1)} copy(bf16[1,128,4096]{2,1,0:T(8,128)(2,1)} %param.10) | data formatting | bytes 2097152 | tf_op args[2]
  45.5 23.3 %reduce.2 = bf16[4096,128]{1,0:T(8,128)(2,1)} reduce(bf16[4096,1,128]{2,1,0:T(2,128)(2,1)S(1)} %bitcast.85, bf16[]{:T(256)} %broadcast.40), dimensions={1}, to_apply=%bitcast.47.reduce_sub_computation | reduce | bytes 2097154
  71.0 8.1 %all-to-all-start.2 = ((bf16[16,2,16384]{2,1,0:T(2,128)(2,1)}), bf16[16,2,16384]{2,1,0:T(2,128)(2,1)}, u32[]{:S(2)}, u32[]{:S(2)}) async-start(bf16[16,2,16384]{2,1,0:T(2,128)(2,1)} %reshape.41), calls=%async_computation.2 | async-start | bytes 2097152 | tf_op jit(solution)/shard_map/all_to_all | solution.py:41
  79.1 5.0 %copy.55 = bf16[1,128,4096]{1,0,2:T(2,128)(2,1)S(1)} copy(bf16[1,128,4096]{2,1,0:T(8,128)(2,1)} %param.8) | data formatting | bytes 2097152 | tf_op args[0]
  84.1 23.3 %reduce = bf16[4096,128]{1,0:T(8,128)(2,1)} reduce(bf16[4096,1,128]{2,1,0:T(2,128)(2,1)S(1)} %bitcast.86, bf16[]{:T(256)} %broadcast.40), dimensions={1}, to_apply=%bitcast.43.reduce_sub_computation | reduce | bytes 2097154
  109.6 8.1 %all-to-all-start = ((bf16[16,2,16384]{2,1,0:T(2,128)(2,1)}), bf16[16,2,16384]{2,1,0:T(2,128)(2,1)}, u32[]{:S(2)}, u32[]{:S(2)}) async-start(bf16[16,2,16384]{2,1,0:T(2,128)(2,1)} %reshape.37), calls=%async_computation | async-start | bytes 2097152 | tf_op jit(solution)/shard_map/all_to_all | solution.py:39
  119.1 5.8 %reshape.40 = bf16[4096,1,128]{2,1,0:T(2,128)(2,1)} reshape(bf16[16,2,16384]{2,1,0:T(2,128)(2,1)} %all-to-all-done.1) | data formatting | bytes 2097152
  129.7 5.8 %reshape.42 = bf16[4096,1,128]{2,1,0:T(2,128)(2,1)} reshape(bf16[16,2,16384]{2,1,0:T(2,128)(2,1)} %all-to-all-done.2) | data formatting | bytes 2097152
  143.8 6.5 %collective-permute-start.1 = (bf16[1,512,256]{2,1,0:T(8,128)(2,1)S(1)}, bf16[1,512,256]{2,1,0:T(8,128)(2,1)S(1)}, u32[]{:S(2)}, u32[]{:S(2)}) collective-permute-start(bf16[1,512,256]{2,1,0:T(8,128)(2,1)S(1)} %slice.9), channel_id=1, source_target_pairs={{0,16},{16,32},{32,48},{48,64},{64,80},{80,96},{96,112},{112,128},... | collective-permute-start | bytes 786440 | tf_op jit(solution)/shard_map/ppermute | solution.py:16
  150.3 4.3 %reshape.38 = bf16[4096,1,128]{2,1,0:T(2,128)(2,1)S(1)} reshape(bf16[16,2,16384]{2,1,0:T(2,128)(2,1)} %all-to-all-done) | data formatting | bytes 2097152
  162.7 2.4 pad_maximum_fusion.1
  165.1 67.0 %while.10 = (s32[]{:T(128)}, bf16[4,512,256]{2,1,0:T(8,128)(2,1)}, pred[2560]{0:T(1024)(128)(4,1)S(1)}, bf16[4,512,2,128]{3,2,1,0:T(2,128)(2,1)S(1)}, bf16[2560,...) while((s32[]{:T(128)}, bf16[4,512,256]{2,1,0:T(8,128)(2,1)}, ...), condition=%wide.region_4.5_spmd, body=%wide.region_0.4_spmd.sunk | while | flops 2037521408 | bytes 28342872 | solution.py:76
  165.3 3.7 %fusion.36 = f32[2,512]{1,0:T(2,128)S(1)} fusion(pred[2560]{0:T(1024)(128)(4,1)S(1)} %get-tuple-element.159, bf16[2560,2,128]{2,0,1:T(8,128)(2,1)S(1)} %get-tuple-element.161, bf16[1,512,2,128]{3,2,1,0:T(2,128)(2,1)S(1)} %constant_dynamic-slice_fusion.2), kind=kOutput, calls=%fused_computation.32.clone.1 | convolution fusion | flops 681576960 | bytes 1579520 | tf_op jit(solution)/shard_map/while/body/eval_jaxpr/sub | solution.py:69
  169.0 5.5 %fusion.37 = f32[2,512,2560]{2,1,0:T(8,128)} fusion(bf16[2560,2,128]{2,0,1:T(8,128)(2,1)S(1)} %get-tuple-element.161, bf16[1,512,2,128]{3,2,1,0:T(2,128)(2,1)S(1)} %constant_dynamic-slice_fusion.2), kind=kOutput, calls=%fused_computation.14.clone.1 | convolution fusion | flops 671088640 | bytes 12058624 | tf_op jit(solution)/shard_map/while/body/eval_jaxpr/qhd,khd->hqk/dot_general | solution.py:64
  174.6 6.3 %multiply_reduce_fusion.2 = (f32[512,2]{0,1:T(2,128)S(1)}, f32[512,2,128]{0,2,1:T(8,128)S(1)}) fusion(bf16[2560,2,128]{0,2,1:T(8,128)(2,1)} %get-tuple-element.162, f32[2,512]{1,0:T(2,128)S(1)} %fusion.36, f32[2,512,2560]{2,1,0:T(8,128)} %fusion.37, pred[2560]{0:T(1024)(128)(4,1)S(1)} %get-tuple-element.159), kind=kOutput, calls=%fused_computation.11.clone.1 | convolution fusion | flops 684460544 | bytes 12331520 | tf_op jit(solution)/shard_map/while/body/eval_jaxpr/hqk,khd->qhd/dot_general | solution.py:71
  182.1 3.7 %fusion.36 = f32[2,512]{1,0:T(2,128)S(1)} fusion(pred[2560]{0:T(1024)(128)(4,1)S(1)} %get-tuple-element.159, bf16[2560,2,128]{2,0,1:T(8,128)(2,1)S(1)} %get-tuple-element.161, bf16[1,512,2,128]{3,2,1,0:T(2,128)(2,1)S(1)} %constant_dynamic-slice_fusion.2), kind=kOutput, calls=%fused_computation.32.clone.1 | convolution fusion | flops 681576960 | bytes 1579520 | tf_op jit(solution)/shard_map/while/body/eval_jaxpr/sub | solution.py:69
  185.8 5.5 %fusion.37 = f32[2,512,2560]{2,1,0:T(8,128)} fusion(bf16[2560,2,128]{2,0,1:T(8,128)(2,1)S(1)} %get-tuple-element.161, bf16[1,512,2,128]{3,2,1,0:T(2,128)(2,1)S(1)} %constant_dynamic-slice_fusion.2), kind=kOutput, calls=%fused_computation.14.clone.1 | convolution fusion | flops 671088640 | bytes 12058624 | tf_op jit(solution)/shard_map/while/body/eval_jaxpr/qhd,khd->hqk/dot_general | solution.py:64
  191.3 6.3 %multiply_reduce_fusion.2 = (f32[512,2]{0,1:T(2,128)S(1)}, f32[512,2,128]{0,2,1:T(8,128)S(1)}) fusion(bf16[2560,2,128]{0,2,1:T(8,128)(2,1)} %get-tuple-element.162, f32[2,512]{1,0:T(2,128)S(1)} %fusion.36, f32[2,512,2560]{2,1,0:T(8,128)} %fusion.37, pred[2560]{0:T(1024)(128)(4,1)S(1)} %get-tuple-element.159), kind=kOutput, calls=%fused_computation.11.clone.1 | convolution fusion | flops 684460544 | bytes 12331520 | tf_op jit(solution)/shard_map/while/body/eval_jaxpr/hqk,khd->qhd/dot_general | solution.py:71
  198.8 3.7 %fusion.36 = f32[2,512]{1,0:T(2,128)S(1)} fusion(pred[2560]{0:T(1024)(128)(4,1)S(1)} %get-tuple-element.159, bf16[2560,2,128]{2,0,1:T(8,128)(2,1)S(1)} %get-tuple-element.161, bf16[1,512,2,128]{3,2,1,0:T(2,128)(2,1)S(1)} %constant_dynamic-slice_fusion.2), kind=kOutput, calls=%fused_computation.32.clone.1 | convolution fusion | flops 681576960 | bytes 1579520 | tf_op jit(solution)/shard_map/while/body/eval_jaxpr/sub | solution.py:69
  202.6 5.5 %fusion.37 = f32[2,512,2560]{2,1,0:T(8,128)} fusion(bf16[2560,2,128]{2,0,1:T(8,128)(2,1)S(1)} %get-tuple-element.161, bf16[1,512,2,128]{3,2,1,0:T(2,128)(2,1)S(1)} %constant_dynamic-slice_fusion.2), kind=kOutput, calls=%fused_computation.14.clone.1 | convolution fusion | flops 671088640 | bytes 12058624 | tf_op jit(solution)/shard_map/while/body/eval_jaxpr/qhd,khd->hqk/dot_general | solution.py:64
  208.1 6.3 %multiply_reduce_fusion.2 = (f32[512,2]{0,1:T(2,128)S(1)}, f32[512,2,128]{0,2,1:T(8,128)S(1)}) fusion(bf16[2560,2,128]{0,2,1:T(8,128)(2,1)} %get-tuple-element.162, f32[2,512]{1,0:T(2,128)S(1)} %fusion.36, f32[2,512,2560]{2,1,0:T(8,128)} %fusion.37, pred[2560]{0:T(1024)(128)(4,1)S(1)} %get-tuple-element.159), kind=kOutput, calls=%fused_computation.11.clone.1 | convolution fusion | flops 684460544 | bytes 12331520 | tf_op jit(solution)/shard_map/while/body/eval_jaxpr/hqk,khd->qhd/dot_general | solution.py:71
  215.6 3.7 %fusion.36 = f32[2,512]{1,0:T(2,128)S(1)} fusion(pred[2560]{0:T(1024)(128)(4,1)S(1)} %get-tuple-element.159, bf16[2560,2,128]{2,0,1:T(8,128)(2,1)S(1)} %get-tuple-element.161, bf16[1,512,2,128]{3,2,1,0:T(2,128)(2,1)S(1)} %constant_dynamic-slice_fusion.2), kind=kOutput, calls=%fused_computation.32.clone.1 | convolution fusion | flops 681576960 | bytes 1579520 | tf_op jit(solution)/shard_map/while/body/eval_jaxpr/sub | solution.py:69
  219.3 5.5 %fusion.37 = f32[2,512,2560]{2,1,0:T(8,128)} fusion(bf16[2560,2,128]{2,0,1:T(8,128)(2,1)S(1)} %get-tuple-element.161, bf16[1,512,2,128]{3,2,1,0:T(2,128)(2,1)S(1)} %constant_dynamic-slice_fusion.2), kind=kOutput, calls=%fused_computation.14.clone.1 | convolution fusion | flops 671088640 | bytes 12058624 | tf_op jit(solution)/shard_map/while/body/eval_jaxpr/qhd,khd->hqk/dot_general | solution.py:64
  224.8 6.3 %multiply_reduce_fusion.2 = (f32[512,2]{0,1:T(2,128)S(1)}, f32[512,2,128]{0,2,1:T(8,128)S(1)}) fusion(bf16[2560,2,128]{0,2,1:T(8,128)(2,1)} %get-tuple-element.162, f32[2,512]{1,0:T(2,128)S(1)} %fusion.36, f32[2,512,2560]{2,1,0:T(8,128)} %fusion.37, pred[2560]{0:T(1024)(128)(4,1)S(1)} %get-tuple-element.159), kind=kOutput, calls=%fused_computation.11.clone.1 | convolution fusion | flops 684460544 | bytes 12331520 | tf_op jit(solution)/shard_map/while/body/eval_jaxpr/hqk,khd->qhd/dot_general | solution.py:71
  232.2 3.2 copy.86
  235.3 11.5 %reduce.3 = bf16[2048,256]{1,0:T(8,128)(2,1)} reduce(bf16[2048,1,256]{2,1,0:T(2,128)(2,1)S(1)} %bitcast.84, bf16[]{:T(256)} %broadcast.40), dimensions={1}, to_apply=%bitcast.58.reduce_sub_computation | reduce | bytes 2097154
  248.2 33.2 %all_to_all.69 = bf16[16,2,16384]{2,1,0:T(2,128)(2,1)} all-to-all(bf16[16,2,16384]{2,1,0:T(2,128)(2,1)S(1)} %reshape.43), channel_id=1, replica_groups=mesh['queue'=32,'seq'=16] {'seq'}, dimensions={0} | all-to-all | bytes 2097152 | tf_op jit(solution)/shard_map/all_to_all | solution.py:34
  281.4 4.3 %reshape.44 = bf16[2048,1,256]{2,1,0:T(2,128)(2,1)S(1)} reshape(bf16[16,2,16384]{2,1,0:T(2,128)(2,1)} %all_to_all.69) | data formatting | bytes 2097152
  290.5 28.9 %collective-permute-done.2 = bf16[1,128,4096]{1,2,0:T(8,128)(2,1)S(1)} collective-permute-done((bf16[1,128,4096]{1,2,0:T(8,128)(2,1)S(1)}, bf16[1,128,4096]{1,2,0:T(8,128)(2,1)S(1)}, u32[]{:S(2)}, u32[]{:S(2)}) %collective-permute-start.2) | collective-permute-done | bytes 1048608 | tf_op jit(solution)/shard_map/ppermute | solution.py:22
  (65 shorter events, 40.2 us)
Async XLA Ops:
  0.0 128.5 %copy-start = (f32[50,4096]{1,0:T(8,128)S(1)}, f32[50,4096]{1,0:T(8,128)}, u32[]{:S(2)}) copy-start(f32[50,4096]{1,0:T(8,128)} %param.11) | copy-start | bytes 2457604
  31.2 39.8 %all-to-all-start.1 = ((bf16[16,2,16384]{2,1,0:T(2,128)(2,1)}), bf16[16,2,16384]{2,1,0:T(2,128)(2,1)}, u32[]{:S(2)}, u32[]{:S(2)}) async-start(bf16[16,2,16384]{2,1,0:T(2,128)(2,1)} %reshape.39), calls=%async_computation.1 | async-start | bytes 2097152 | tf_op jit(solution)/shard_map/all_to_all | solution.py:40
  71.0 38.6 %all-to-all-start.2 = ((bf16[16,2,16384]{2,1,0:T(2,128)(2,1)}), bf16[16,2,16384]{2,1,0:T(2,128)(2,1)}, u32[]{:S(2)}, u32[]{:S(2)}) async-start(bf16[16,2,16384]{2,1,0:T(2,128)(2,1)} %reshape.41), calls=%async_computation.2 | async-start | bytes 2097152 | tf_op jit(solution)/shard_map/all_to_all | solution.py:41
  109.6 40.7 %all-to-all-start = ((bf16[16,2,16384]{2,1,0:T(2,128)(2,1)}), bf16[16,2,16384]{2,1,0:T(2,128)(2,1)}, u32[]{:S(2)}, u32[]{:S(2)}) async-start(bf16[16,2,16384]{2,1,0:T(2,128)(2,1)} %reshape.37), calls=%async_computation | async-start | bytes 2097152 | tf_op jit(solution)/shard_map/all_to_all | solution.py:39
  127.1 32.4 %collective-permute-start = (bf16[1,512,256]{2,1,0:T(8,128)(2,1)S(1)}, bf16[1,512,256]{2,1,0:T(8,128)(2,1)S(1)}, u32[]{:S(2)}, u32[]{:S(2)}) collective-permute-start(bf16[1,512,256]{2,1,0:T(8,128)(2,1)S(1)} %slice.8), channel_id=1, source_target_pairs={{0,16},{16,32},{32,48},{48,64},{64,80},{80,96},{96,112},{112,128},... | collective-permute-start | bytes 786440 | tf_op jit(solution)/shard_map/ppermute | solution.py:16
  140.2 1.4 copy-start.3
  143.8 18.8 %collective-permute-start.1 = (bf16[1,512,256]{2,1,0:T(8,128)(2,1)S(1)}, bf16[1,512,256]{2,1,0:T(8,128)(2,1)S(1)}, u32[]{:S(2)}, u32[]{:S(2)}) collective-permute-start(bf16[1,512,256]{2,1,0:T(8,128)(2,1)S(1)} %slice.9), channel_id=1, source_target_pairs={{0,16},{16,32},{32,48},{48,64},{64,80},{80,96},{96,112},{112,128},... | collective-permute-start | bytes 786440 | tf_op jit(solution)/shard_map/ppermute | solution.py:16
  155.8 3.9 %copy-start.2 = (bf16[2048,2,128]{0,2,1:T(8,128)(2,1)S(1)}, bf16[2048,2,128]{0,2,1:T(8,128)(2,1)}, u32[]{:S(2)}) copy-start(bf16[2048,2,128]{0,2,1:T(8,128)(2,1)} %concatenate.21) | copy-start | bytes 3145732
  285.8 34.9 %copy-start.1 = (f32[50,4096]{1,0:T(8,128)S(1)}, f32[50,4096]{1,0:T(8,128)}, u32[]{:S(2)}) copy-start(f32[50,4096]{1,0:T(8,128)} %param.11) | copy-start | bytes 2457604
  288.5 30.9 %collective-permute-start.2 = (bf16[1,128,4096]{1,2,0:T(8,128)(2,1)S(1)}, bf16[1,128,4096]{1,2,0:T(8,128)(2,1)S(1)}, u32[]{:S(2)}, u32[]{:S(2)}) collective-permute-start(bf16[1,128,4096]{1,2,0:T(8,128)(2,1)S(1)} %bitcast.94), channel_id=1, source_target_pairs={{0,16},{16,32},{32,48},{48,64},{64,80},{80,96},{96,112},{112,128},... | collective-permute-start | bytes 3145736 | tf_op jit(solution)/shard_map/ppermute | solution.py:22
where the time goes:
time: 325 us; the launch traced here: 321 us
  other arithmetic  85.6 us (26%)
  local copies, waits for them, and re-layouts  73.4 us (23%)
  matrix products  62.7 us (19%)
  starting transfers between devices  35.2 us (11%)
  blocking collectives  33.2 us (10%)
  waiting for transfers between devices  28.9 us (9%)
    unnamed x4, other arithmetic  81.6 us
    unnamed x24, local copies, waits for them, and re-layouts  49.6 us
    all_to_all x1, blocking collectives, back_exchange(): lax.all_to_all(normed, 'seq', split_axis=1, concat_axis=2, tiled=True)  33.2 us
    ppermute x1, waiting for transfers between devices, shifted(): return lax.ppermute(value, axis, pairs)  28.9 us
    dot_general x4, matrix products, attend_block(): jnp.einsum('hqk,khd->qhd', weights, all_values, preferred_element_type=jn...  25.3 us
    dot_general x4, matrix products, attend_block(): jnp.einsum('qhd,khd->hqk', query_block, all_keys, preferred_element_type=...  22.1 us
    sub x4, matrix products, attend_block(): expon = jnp.exp(scores - top_score)  14.9 us
    all_to_all x1, starting transfers between devices, per_device(): lax.all_to_all(key_rows, 'seq', split_axis=2, concat_axis=1, tiled=True)  9.29 us
  transfers between devices with their start and end apart: 6, of which 1 were waited for; matrix products, arithmetic and copies ran while one was open for 30% of the time, Pallas kernels for 0%

commit v1 on v0

v1 whole, which is shorter than its diff:
```python
import functools
import math

import jax
import jax.numpy as jnp
from jax import lax
from jax.experimental import pallas as pl
from jax.experimental.pallas import tpu as pltpu
from jax.sharding import PartitionSpec as P

HEADS_DEV = 2
HD = 128
FTOK = 128
HALO = 4
LEVELS = 50
EDGE = HALO * FTOK
MESH = pl.DeviceIdType.MESH
EXP2_SCALE = HD**-0.5 * math.log2(math.e)


def kernel(
    nq,
    ns,
    q_ref,
    k_ref,
    v_ref,
    gains_ref,
    level_ref,
    halo_ref,
    out_ref,
    qbuf,
    kbuf,
    vbuf,
    obuf,
    gbuf,
    q_send,
    k_send,
    v_send,
    q_recv,
    k_recv,
    v_recv,
    halo_send,
    halo_recv,
    out_send,
    out_recv,
    gain_sem,
    ready_sem,
):
    tok = q_ref.shape[0]
    width = HEADS_DEV * HD
    tail = EDGE // tok
    me_q = lax.axis_index("queue")
    me = lax.axis_index("seq")
    nxt = lax.rem(me_q + 1, nq)
    prv = lax.rem(me_q + nq - 1, nq)

    barrier = pltpu.get_barrier_semaphore()

    @pl.loop(1, ns)
    def _(step):
        pl.semaphore_signal(
            barrier, inc=1, device_id=(me_q, lax.rem(me + step, ns)), device_id_type=MESH
        )

    pl.semaphore_signal(barrier, inc=1, device_id=(nxt, me), device_id_type=MESH)
    pl.semaphore_signal(barrier, inc=1, device_id=(prv, me), device_id_type=MESH)

    gain_copy = pltpu.make_async_copy(
        gains_ref.at[:, pl.ds(pl.multiple_of(me * width, width), width)], gbuf, gain_sem
    )
    gain_copy.start()
    pl.semaphore_wait(barrier, ns + 1)

    is_tail = (me >= ns - tail).astype(jnp.int32)

    def kv_dst(buf, h, source):
        return buf.at[h, pl.ds(pl.multiple_of(EDGE + source * tok, tok), tok)]

    def q_dst(h, source):
        return qbuf.at[h, pl.ds(pl.multiple_of(source * tok, tok), tok)]

    def src(ref, h, target):
        return ref.at[:, pl.ds(pl.multiple_of(target * width + h * HD, HD), HD)]

    @pl.loop(0, HEADS_DEV)
    def _(h):
        pltpu.make_async_copy(src(k_ref, h, me), kv_dst(kbuf, h, me), k_recv.at[h, is_tail]).start()
        pltpu.make_async_copy(src(v_ref, h, me), kv_dst(vbuf, h, me), v_recv.at[h, is_tail]).start()
        pltpu.make_async_copy(src(q_ref, h, me), q_dst(h, me), q_recv.at[h, me]).start()

        @pl.loop(1, ns)
        def _(step):
            peer = lax.rem(me + step, ns)
            pltpu.make_async_remote_copy(
                src(k_ref, h, peer), kv_dst(kbuf, h, me), k_send, k_recv.at[h, is_tail],
                device_id=(me_q, peer), device_id_type=MESH,
            ).start()

        @pl.loop(1, ns)
        def _(step):
            peer = lax.rem(me + step, ns)
            pltpu.make_async_remote_copy(
                src(v_ref, h, peer), kv_dst(vbuf, h, me), v_send, v_recv.at[h, is_tail],
                device_id=(me_q, peer), device_id_type=MESH,
            ).start()

        @pl.loop(1, ns)
        def _(step):
            peer = lax.rem(me + step, ns)
            pltpu.make_async_remote_copy(
                src(q_ref, h, peer), q_dst(h, me), q_send, q_recv.at[h, me],
                device_id=(me_q, peer), device_id_type=MESH,
            ).start()

    pl.semaphore_signal(ready_sem, inc=1, device_id=(prv, me), device_id_type=MESH)

    gain_copy.wait()
    gain_row = gbuf[pl.ds(level_ref[0], 1), :]
    first_seen = jnp.where(me_q > 0, HALO - halo_ref[0], HALO)
    frames = lax.broadcasted_iota(jnp.int32, (1, EDGE), 1) // FTOK
    bias = jnp.where(frames >= first_seen, jnp.float32(0), jnp.float32(-1e30))

    def wait_rows(sem, buf, h, first, rows):
        part = buf.at[h, pl.ds(first, rows)]
        pltpu.make_async_copy(part, part, sem).wait()

    def halo_copy(buf, h, i):
        return pltpu.make_async_remote_copy(
            buf.at[h, pl.ds(ns * tok, EDGE)], buf.at[h, pl.ds(0, EDGE)],
            halo_send.at[i, h], halo_recv.at[i, h],
            device_id=(nxt, me), device_id_type=MESH,
        )

    pl.semaphore_wait(ready_sem, 1)

    rows = 2 * tok

    for h in range(HEADS_DEV):
        for i, (buf, recv) in enumerate(((kbuf, k_recv), (vbuf, v_recv))):
            wait_rows(recv.at[h, 1], buf, h, ns * tok, EDGE)
            halo_copy(buf, h, i).start()
        for i, (buf, recv) in enumerate(((kbuf, k_recv), (vbuf, v_recv))):
            wait_rows(recv.at[h, 0], buf, h, EDGE, ns * tok - EDGE)
            halo_copy(buf, h, i).wait_recv()
        gain_head = gain_row[:, h * HD : (h + 1) * HD]

        @pl.loop(0, ns // 2)
        def _(step):
            pair = lax.rem(me // 2 + ns // 2 - step, ns // 2)
            first = pl.multiple_of(pair * rows, rows)
            for j in range(2):
                peer = 2 * pair + j
                pltpu.make_async_copy(q_dst(h, peer), q_dst(h, peer), q_recv.at[h, peer]).wait()
            queries = qbuf[h, pl.ds(first, rows), :]
            scores = lax.dot_general(
                queries, kbuf[h], (((1,), (1,)), ((), ())), preferred_element_type=jnp.float32
            )
            edge = scores[:, :EDGE] + bias
            own = scores[:, EDGE:]
            top = jnp.maximum(
                jnp.max(edge, axis=1, keepdims=True), jnp.max(own, axis=1, keepdims=True)
            )
            edge_w = jnp.exp2((edge - top) * EXP2_SCALE)
            own_w = jnp.exp2((own - top) * EXP2_SCALE)
            total = jnp.sum(edge_w, axis=1, keepdims=True) + jnp.sum(own_w, axis=1, keepdims=True)
            mixed = jnp.dot(
                edge_w.astype(jnp.bfloat16), vbuf[h, :EDGE], preferred_element_type=jnp.float32
            ) + jnp.dot(
                own_w.astype(jnp.bfloat16), vbuf[h, EDGE:], preferred_element_type=jnp.float32
            )
            mixed = mixed / total
            mean_sq = jnp.mean(mixed * mixed, axis=1, keepdims=True)
            normed = mixed * lax.rsqrt(mean_sq + 1e-06) * gain_head
            obuf[h, pl.ds(first, rows), :] = normed.astype(jnp.bfloat16)
            for j in range(2):
                peer = 2 * pair + j
                pltpu.make_async_remote_copy(
                    obuf.at[h, pl.ds(pl.multiple_of(peer * tok, tok), tok)],
                    out_ref.at[:, pl.ds(pl.multiple_of(me * width + h * HD, HD), HD)],
                    out_send, out_recv,
                    device_id=(nxt, peer), device_id_type=MESH,
                ).start()

    for ref, sem in ((q_ref, q_send), (k_ref, k_send), (v_ref, v_send)):
        sent = ref.at[:, pl.ds(0, (ns - 1) * width)]
        pltpu.make_async_copy(sent, sent, sem).wait()
    for h in range(HEADS_DEV):
        for i, buf in enumerate((kbuf, vbuf)):
            halo_copy(buf, h, i).wait_send()
    pltpu.make_async_copy(out_ref, out_ref, out_send).wait()
    pltpu.make_async_copy(out_ref, out_ref, out_recv).wait()


def per_device(query_rows, key_rows, value_rows, level_gains, noise_levels, halo_frames):
    nq, ns = lax.axis_size("queue"), lax.axis_size("seq")
    _, tok, features = query_rows.shape
    group = ns * tok
    flops = 4 * HEADS_DEV * group * (group + EDGE) * HD
    dma = pltpu.SemaphoreType.DMA
    out = pl.pallas_call(
        functools.partial(kernel, nq, ns),
        out_shape=jax.ShapeDtypeStruct((tok, features), jnp.bfloat16),
        in_specs=[pl.BlockSpec(memory_space=pl.ANY)] * 4
        + [pl.BlockSpec(memory_space=pltpu.SMEM)] * 2,
        out_specs=pl.BlockSpec(memory_space=pl.ANY),
        scratch_shapes=[
            pltpu.VMEM((HEADS_DEV, group, HD), jnp.bfloat16),
            pltpu.VMEM((HEADS_DEV, EDGE + group, HD), jnp.bfloat16),
            pltpu.VMEM((HEADS_DEV, EDGE + group, HD), jnp.bfloat16),
            pltpu.VMEM((HEADS_DEV, group, HD), jnp.bfloat16),
            pltpu.VMEM((LEVELS, HEADS_DEV * HD), jnp.float32),
            dma, dma, dma,
            dma((HEADS_DEV, ns)),
            dma((HEADS_DEV, 2)),
            dma((HEADS_DEV, 2)),
            dma((2, HEADS_DEV)),
            dma((2, HEADS_DEV)),
            dma, dma, dma,
            pltpu.SemaphoreType.REGULAR,
        ],
        compiler_params=pltpu.CompilerParams(
            collective_id=0, has_side_effects=True, vmem_limit_bytes=56 * 2**20
        ),
        cost_estimate=pl.CostEstimate(
            flops=flops, bytes_accessed=8 * 2**20, transcendentals=HEADS_DEV * group * (group + EDGE)
        ),
    )(
        query_rows.reshape(tok, features),
        key_rows.reshape(tok, features),
        value_rows.reshape(tok, features),
        level_gains,
        noise_levels,
        halo_frames,
    )
    return out.reshape(1, tok, features)


def solution(mesh):
    placed = (
        P("queue", "seq", None),
        P("queue", "seq", None),
        P("queue", "seq", None),
        P(),
        P("queue"),
        P("queue"),
    )
    return jax.shard_map(
        per_device, mesh=mesh, in_specs=placed, out_specs=P("queue", "seq", None), check_vma=False
    )
```

time: 325 us -> 114 us (0.35); the launches traced: 321 us -> 114 us
  Pallas kernels: 0 us -> 110 us
  other arithmetic: 85.6 us -> 0 us
  local copies, waits for them, and re-layouts: 73.4 us -> 2.29 us
  matrix products: 62.7 us -> 0 us
  starting transfers between devices: 35.2 us -> 0 us
  blocking collectives: 33.2 us -> 0 us
  waiting for transfers between devices: 28.9 us -> 0 us
    pallas_call x0 -> x1, Pallas kernels: none -> 110 us  [per_device(): pl.pallas_call(functools.partial(kernel, nq, ns), out_shape=jax.ShapeDtyp...]
    unnamed x4 -> x0, other arithmetic: 81.6 us -> none
    dot_general x9 -> x0, matrix products: 47.8 us -> none  [the longest x4 25.3 us: attend_block(): jnp.einsum('hqk,khd->qhd', weights, all_values, preferred_element_type=jn...]
    unnamed x24 -> x1, local copies, waits for them, and re-layouts: 49.6 us -> 2.29 us
    all_to_all x1 -> x0, blocking collectives: 33.2 us -> none  [back_exchange(): lax.all_to_all(normed, 'seq', split_axis=1, concat_axis=2, tiled=True)]
    ppermute x3 -> x0, waiting for transfers between devices: 28.9 us -> none  [the longest x1 28.9 us: shifted(): return lax.ppermute(value, axis, pairs)]
    all_to_all x3 -> x0, starting transfers between devices: 25.5 us -> none  [the longest x1 9.29 us: per_device(): lax.all_to_all(key_rows, 'seq', split_axis=2, concat_axis=1, tiled=True)]
    sub x4 -> x0, matrix products: 14.9 us -> none  [attend_block(): expon = jnp.exp(scores - top_score)]
  transfers between devices with their start and end apart: 6 -> 0, of which waited for: 1 -> 0; matrix products, arithmetic and copies ran while one was open for 30% -> 0% of each run, Pallas kernels for 0% -> 0%
where the time goes in v1:
time: 114 us
  Pallas kernels  110 us (96%)
  local copies, waits for them, and re-layouts  2.29 us (2%)
  between operations  1.3 us (1%)
    pallas_call x1, Pallas kernels, per_device(): pl.pallas_call(functools.partial(kernel, nq, ns), out_shape=jax.ShapeDtyp...  110 us
    unnamed x1, local copies, waits for them, and re-layouts  2.29 us

profile of v1, /device:TPU:56, one launch (start us, length us, event | category | flops | bytes accessed | tf_op | source)
XLA Modules:
  0.0 113.6 jit_solution(15557170646007132923)
XLA Ops:
  1.3 110.0 %shard_map.64 = bf16[128,4096]{1,0:T(8,128)(2,1)} custom-call(bf16[128,4096]{1,0:T(8,128)(2,1)} %bitcast.5, bf16[128,4096]{1,0:T(8,128)(2,1)} %bitcast.6, bf16[128,4096]{1,0:T(8,128)(2,1)} %bitcast.7, f32[50,4096]{1,0:T(8,128)} %gains_ref.1, s32[1]{0:T(128)S(6)} %copy.8.level_ref, s32[1]{0:T(128)S(6)} %copy.9.halo_ref), custom_call_target="tpu_custom_call" | custom-call | flops 5368709120 | bytes 8388608 | tf_op jit(solution)/shard_map/pallas_call | solution.py:200
  111.3 2.3 %copy.10 = bf16[1,128,4096]{2,1,0:T(8,128)(2,1)} copy(bf16[1,128,4096]{2,1,0:T(8,128)(2,1)} %bitcast.4) | data formatting | bytes 2097152

commit v2 on v1

v2 whole, which is shorter than its diff:
```python
import functools
import math

import jax
import jax.numpy as jnp
from jax import lax
from jax.experimental import pallas as pl
from jax.experimental.pallas import tpu as pltpu
from jax.sharding import PartitionSpec as P

HEADS_DEV = 2
HD = 128
FTOK = 128
HALO = 4
LEVELS = 50
EDGE = HALO * FTOK
STAR = 0
MESH = pl.DeviceIdType.MESH
EXP2_SCALE = HD**-0.5 * math.log2(math.e)


def kernel(
    nq,
    ns,
    q_ref,
    k_ref,
    v_ref,
    gains_ref,
    level_ref,
    halo_ref,
    out_ref,
    qbuf,
    kbuf,
    vbuf,
    obuf,
    gbuf,
    q_send,
    k_send,
    v_send,
    q_recv,
    k_recv,
    v_recv,
    halo_send,
    halo_recv,
    out_send,
    out_recv,
    gain_sem,
    ready_sem,
    star_sem,
):
    tok = q_ref.shape[0]
    width = HEADS_DEV * HD
    tail = EDGE // tok
    me_q = lax.axis_index("queue")
    me = lax.axis_index("seq")
    nxt = lax.rem(me_q + 1, nq)
    prv = lax.rem(me_q + nq - 1, nq)

    barrier = pltpu.get_barrier_semaphore()
    is_star = me == STAR

    @pl.loop(1, ns)
    def _(step):
        peer = lax.rem(me + step, ns)

        @pl.when(peer != STAR)
        def _():
            pl.semaphore_signal(barrier, inc=1, device_id=(me_q, peer), device_id_type=MESH)

    gain_copy = pltpu.make_async_copy(
        gains_ref.at[:, pl.ds(pl.multiple_of(me * width, width), width)], gbuf, gain_sem
    )
    gain_copy.start()

    @pl.when(is_star)
    def _():
        pl.semaphore_signal(barrier, inc=1, device_id=(nxt, STAR), device_id_type=MESH)
        pl.semaphore_wait(star_sem, ns - 1)

    @pl.when(jnp.logical_not(is_star))
    def _():
        pl.semaphore_wait(barrier, ns - 1)
        pl.semaphore_signal(star_sem, inc=1, device_id=(me_q, STAR), device_id_type=MESH)

    is_tail = (me >= ns - tail).astype(jnp.int32)
    ny = ns // 2
    row, side = me // 2, lax.rem(me, 2)

    def offset(step):
        return jnp.where(lax.rem(step, 2) == 1, (step + 1) // 2, ny - step // 2)

    def kv_dst(buf, h, source):
        return buf.at[h, pl.ds(pl.multiple_of(EDGE + source * tok, tok), tok)]

    def q_dst(buf, h, source):
        return buf.at[h, pl.ds(pl.multiple_of(source * tok, tok), tok)]

    def src(ref, h, target):
        return ref.at[:, pl.ds(pl.multiple_of(target * width + h * HD, HD), HD)]

    def send(ref, buf, dst, sem, done, h, peer):
        pltpu.make_async_remote_copy(
            src(ref, h, peer), dst(buf, h, me), sem, done, device_id=(me_q, peer), device_id_type=MESH
        ).start()

    def send_pair(ref, buf, dst, sem, done, h, step):
        pair = lax.rem(row + offset(step), ny)
        send(ref, buf, dst, sem, done, h, 2 * pair + side)
        send(ref, buf, dst, sem, done, h, 2 * pair + 1 - side)

    def send_first(ref, buf, dst, sem, done, h):
        pltpu.make_async_copy(src(ref, h, me), dst(buf, h, me), done).start()
        send(ref, buf, dst, sem, done, h, 2 * row + 1 - side)

    def parts(h):
        return (
            (k_ref, kbuf, kv_dst, k_send, k_recv.at[h, is_tail], h),
            (v_ref, vbuf, kv_dst, v_send, v_recv.at[h, is_tail], h),
            (q_ref, qbuf, q_dst, q_send, q_recv.at[h, me], h),
        )

    def send_all(part):
        send_first(*part)

        @pl.loop(1, ny)
        def _(step):
            send_pair(*part, step)

    (keys0, values0, queries0), (keys1, values1, queries1) = parts(0), parts(1)
    send_all(keys0)
    send_all(values0)

    @pl.when(is_star)
    def _():
        pl.semaphore_wait(barrier, 1)
        pl.semaphore_signal(ready_sem, inc=1, device_id=(prv, STAR), device_id_type=MESH)
        pl.semaphore_wait(ready_sem, 1)

        @pl.loop(1, ns)
        def _(step):
            pl.semaphore_signal(
                ready_sem, inc=1, device_id=(me_q, lax.rem(me + step, ns)), device_id_type=MESH
            )

    @pl.when(jnp.logical_not(is_star))
    def _():
        pl.semaphore_wait(ready_sem, 1)

    gain_copy.wait()
    gain_row = gbuf[pl.ds(level_ref[0], 1), :]
    first_seen = jnp.where(me_q > 0, HALO - halo_ref[0], HALO)
    frames = lax.broadcasted_iota(jnp.int32, (1, EDGE), 1) // FTOK
    bias = jnp.where(frames >= first_seen, jnp.float32(0), jnp.float32(-1e30))

    def wait_rows(sem, buf, h, first, rows):
        part = buf.at[h, pl.ds(first, rows)]
        pltpu.make_async_copy(part, part, sem).wait()

    def halo_copy(buf, h, i):
        return pltpu.make_async_remote_copy(
            buf.at[h, pl.ds(ns * tok, EDGE)], buf.at[h, pl.ds(0, EDGE)],
            halo_send.at[i, h], halo_recv.at[i, h],
            device_id=(nxt, me), device_id_type=MESH,
        )

    rows = 2 * tok

    def place(step):
        pair = lax.rem(row + 2 * ny - offset(step), ny)
        return pair, pl.multiple_of(pair * rows, rows)

    def forward_halo(h, i):
        buf, recv = ((kbuf, k_recv), (vbuf, v_recv))[i]
        wait_rows(recv.at[h, 1], buf, h, ns * tok, EDGE)
        halo_copy(buf, h, i).start()

    def wait_keys(h):
        for i, (buf, recv) in enumerate(((kbuf, k_recv), (vbuf, v_recv))):
            wait_rows(recv.at[h, 0], buf, h, EDGE, ns * tok - EDGE)
            halo_copy(buf, h, i).wait_recv()

    def attend(h, step):
        pair, first = place(step)
        for j in range(2):
            part = q_dst(qbuf, h, 2 * pair + j)
            pltpu.make_async_copy(part, part, q_recv.at[h, 2 * pair + j]).wait()
        queries = qbuf[h, pl.ds(first, rows), :]
        scores = lax.dot_general(
            queries, kbuf[h], (((1,), (1,)), ((), ())), preferred_element_type=jnp.float32
        )
        edge = scores[:, :EDGE] + bias
        own = scores[:, EDGE:]
        top = jnp.maximum(
            jnp.max(edge, axis=1, keepdims=True), jnp.max(own, axis=1, keepdims=True)
        )
        edge_w = jnp.exp2((edge - top) * EXP2_SCALE)
        own_w = jnp.exp2((own - top) * EXP2_SCALE)
        total = jnp.sum(edge_w, axis=1, keepdims=True) + jnp.sum(own_w, axis=1, keepdims=True)
        mixed = jnp.dot(
            edge_w.astype(jnp.bfloat16), vbuf[h, :EDGE], preferred_element_type=jnp.float32
        ) + jnp.dot(
            own_w.astype(jnp.bfloat16), vbuf[h, EDGE:], preferred_element_type=jnp.float32
        )
        mixed = mixed / total
        mean_sq = jnp.mean(mixed * mixed, axis=1, keepdims=True)
        normed = mixed * lax.rsqrt(mean_sq + 1e-06) * gain_row[:, h * HD : (h + 1) * HD]
        obuf[h, pl.ds(first, rows), :] = normed.astype(jnp.bfloat16)

    def send_out(h, step):
        pair, _ = place(step)
        for j in range(2):
            peer = 2 * pair + j
            pltpu.make_async_remote_copy(
                obuf.at[h, pl.ds(pl.multiple_of(peer * tok, tok), tok)],
                out_ref.at[:, pl.ds(pl.multiple_of(me * width + h * HD, HD), HD)],
                out_send, out_recv,
                device_id=(nxt, peer), device_id_type=MESH,
            ).start()

    forward_halo(0, 0)
    send_all(keys1)
    forward_halo(0, 1)
    send_all(values1)
    forward_halo(1, 0)
    send_all(queries0)
    forward_halo(1, 1)
    send_all(queries1)

    for h in range(HEADS_DEV):
        wait_keys(h)

        @pl.loop(0, ny)
        def _(step):
            attend(h, step)
            send_out(h, step)

    for ref, sem in ((q_ref, q_send), (k_ref, k_send), (v_ref, v_send)):
        sent = ref.at[:, pl.ds(0, (ns - 1) * width)]
        pltpu.make_async_copy(sent, sent, sem).wait()
    for h in range(HEADS_DEV):
        for i, buf in enumerate((kbuf, vbuf)):
            halo_copy(buf, h, i).wait_send()
    pltpu.make_async_copy(out_ref, out_ref, out_send).wait()
    pltpu.make_async_copy(out_ref, out_ref, out_recv).wait()


def per_device(query_rows, key_rows, value_rows, level_gains, noise_levels, halo_frames):
    nq, ns = lax.axis_size("queue"), lax.axis_size("seq")
    _, tok, features = query_rows.shape
    group = ns * tok
    flops = 4 * HEADS_DEV * group * (group + EDGE) * HD
    dma = pltpu.SemaphoreType.DMA
    out = pl.pallas_call(
        functools.partial(kernel, nq, ns),
        out_shape=pltpu.VMEM((tok, features), jnp.bfloat16),
        in_specs=[pl.BlockSpec(memory_space=pl.ANY)] * 4
        + [pl.BlockSpec(memory_space=pltpu.SMEM)] * 2,
        out_specs=pl.BlockSpec(memory_space=pl.ANY),
        scratch_shapes=[
            pltpu.VMEM((HEADS_DEV, group, HD), jnp.bfloat16),
            pltpu.VMEM((HEADS_DEV, EDGE + group, HD), jnp.bfloat16),
            pltpu.VMEM((HEADS_DEV, EDGE + group, HD), jnp.bfloat16),
            pltpu.VMEM((HEADS_DEV, group, HD), jnp.bfloat16),
            pltpu.VMEM((LEVELS, HEADS_DEV * HD), jnp.float32),
            dma, dma, dma,
            dma((HEADS_DEV, ns)),
            dma((HEADS_DEV, 2)),
            dma((HEADS_DEV, 2)),
            dma((2, HEADS_DEV)),
            dma((2, HEADS_DEV)),
            dma, dma, dma,
            pltpu.SemaphoreType.REGULAR,
            pltpu.SemaphoreType.REGULAR,
        ],
        compiler_params=pltpu.CompilerParams(
            collective_id=0, has_side_effects=True, vmem_limit_bytes=56 * 2**20
        ),
        cost_estimate=pl.CostEstimate(
            flops=flops, bytes_accessed=8 * 2**20, transcendentals=HEADS_DEV * group * (group + EDGE)
        ),
    )(
        query_rows.reshape(tok, features),
        key_rows.reshape(tok, features),
        value_rows.reshape(tok, features),
        level_gains,
        noise_levels,
        halo_frames,
    )
    return out.reshape(1, tok, features)


def solution(mesh):
    placed = (
        P("queue", "seq", None),
        P("queue", "seq", None),
        P("queue", "seq", None),
        P(),
        P("queue"),
        P("queue"),
    )
    return jax.shard_map(
        per_device, mesh=mesh, in_specs=placed, out_specs=P("queue", "seq", None), check_vma=False
    )
```

time: 114 us -> 111 us (0.974); the launches traced: 114 us -> 109 us
  Pallas kernels: 110 us -> 107 us
  local copies, waits for them, and re-layouts: 2.29 us -> 0.97 us
    pallas_call x1, Pallas kernels: 110 us -> 107 us  [per_device(): pl.pallas_call(functools.partial(kernel, nq, ns), out_shape=pltpu.VMEM((t...]
    unnamed x1, local copies, waits for them, and re-layouts: 2.29 us -> 0.97 us
where the time goes in v2:
time: 111 us; the launch traced here: 109 us
  Pallas kernels  107 us (96%)
  between operations  1.3 us (1%)
    pallas_call x1, Pallas kernels, per_device(): pl.pallas_call(functools.partial(kernel, nq, ns), out_shape=pltpu.VMEM((t...  107 us

profile of v2, /device:TPU:56, one launch (start us, length us, event | category | flops | bytes accessed | tf_op | source)
XLA Modules:
  0.0 109.4 jit_solution(11748547331847848400)
XLA Ops:
  1.3 107.1 %shard_map.64 = bf16[128,4096]{1,0:T(8,128)(2,1)S(1)} custom-call(bf16[128,4096]{1,0:T(8,128)(2,1)} %bitcast.5, bf16[128,4096]{1,0:T(8,128)(2,1)} %bitcast.6, bf16[128,4096]{1,0:T(8,128)(2,1)} %bitcast.7, f32[50,4096]{1,0:T(8,128)} %gains_ref.1, s32[1]{0:T(128)S(6)} %copy.9.level_ref, s32[1]{0:T(128)S(6)} %copy.10.halo_ref), custom_call_target="tpu_custom_call" | custom-call | flops 5368709120 | bytes 8388608 | tf_op jit(solution)/shard_map/pallas_call | solution.py:253
  108.4 1.0 copy.8

commit v3 on v2

--- a/solution.py
+++ b/solution.py
@@ -15,6 +15,9 @@
 LEVELS = 50
 EDGE = HALO * FTOK
 STAR = 0
+RUN = 4
+TURNS = (0, 2, 6, 4, 3, 5, 1, 7)
+KEY_BLOCK = 1024
 MESH = pl.DeviceIdType.MESH
 EXP2_SCALE = HD**-0.5 * math.log2(math.e)
 
@@ -47,6 +50,7 @@
     gain_sem,
     ready_sem,
     star_sem,
+    go_sem,
 ):
     tok = q_ref.shape[0]
     width = HEADS_DEV * HD
@@ -87,7 +91,7 @@
     row, side = me // 2, lax.rem(me, 2)
 
     def offset(step):
-        return jnp.where(lax.rem(step, 2) == 1, (step + 1) // 2, ny - step // 2)
+        return sum(jnp.where(step == i, turn, 0) for i, turn in enumerate(TURNS))
 
     def kv_dst(buf, h, source):
         return buf.at[h, pl.ds(pl.multiple_of(EDGE + source * tok, tok), tok)]
@@ -164,6 +168,7 @@
         )
 
     rows = 2 * tok
+    keys_all = EDGE + ns * tok
 
     def place(step):
         pair = lax.rem(row + 2 * ny - offset(step), ny)
@@ -180,31 +185,37 @@
             halo_copy(buf, h, i).wait_recv()
 
     def attend(h, step):
-        pair, first = place(step)
-        for j in range(2):
-            part = q_dst(qbuf, h, 2 * pair + j)
-            pltpu.make_async_copy(part, part, q_recv.at[h, 2 * pair + j]).wait()
-        queries = qbuf[h, pl.ds(first, rows), :]
-        scores = lax.dot_general(
-            queries, kbuf[h], (((1,), (1,)), ((), ())), preferred_element_type=jnp.float32
-        )
-        edge = scores[:, :EDGE] + bias
-        own = scores[:, EDGE:]
-        top = jnp.maximum(
-            jnp.max(edge, axis=1, keepdims=True), jnp.max(own, axis=1, keepdims=True)
-        )
-        edge_w = jnp.exp2((edge - top) * EXP2_SCALE)
-        own_w = jnp.exp2((own - top) * EXP2_SCALE)
-        total = jnp.sum(edge_w, axis=1, keepdims=True) + jnp.sum(own_w, axis=1, keepdims=True)
-        mixed = jnp.dot(
-            edge_w.astype(jnp.bfloat16), vbuf[h, :EDGE], preferred_element_type=jnp.float32
-        ) + jnp.dot(
-            own_w.astype(jnp.bfloat16), vbuf[h, EDGE:], preferred_element_type=jnp.float32
-        )
-        mixed = mixed / total
+        firsts = []
+        for i in range(2):
+            pair, first = place(2 * step + i)
+            firsts.append(first)
+            for j in range(2):
+                part = q_dst(qbuf, h, 2 * pair + j)
+                pltpu.make_async_copy(part, part, q_recv.at[h, 2 * pair + j]).wait()
+        queries = jnp.concatenate([qbuf[h, pl.ds(first, rows), :] for first in firsts], axis=0)
+        acc = top = None
+        for start in range(0, keys_all, KEY_BLOCK):
+            size = min(KEY_BLOCK, keys_all - start)
+            scores = lax.dot_general(
+                queries, kbuf[h, start : start + size], (((1,), (1,)), ((), ())),
+                preferred_element_type=jnp.float32,
+            )
+            if start == 0:
+                scores = jnp.concatenate([scores[:, :EDGE] + bias, scores[:, EDGE:]], axis=1)
+            peak = jnp.max(scores, axis=1, keepdims=True)
+            new_top = peak if top is None else jnp.maximum(top, peak)
+            weights = jnp.exp2((scores - new_top) * EXP2_SCALE).astype(jnp.bfloat16)
+            values = jnp.concatenate(
+                [vbuf[h, start : start + size], jnp.ones((size, HD), jnp.bfloat16)], axis=1
+            )
+            part = jnp.dot(weights, values, preferred_element_type=jnp.float32)
+            acc = part if acc is None else acc * jnp.exp2((top - new_top) * EXP2_SCALE) + part
+            top = new_top
+        mixed = acc[:, :HD] / acc[:, HD:]
         mean_sq = jnp.mean(mixed * mixed, axis=1, keepdims=True)
         normed = mixed * lax.rsqrt(mean_sq + 1e-06) * gain_row[:, h * HD : (h + 1) * HD]
-        obuf[h, pl.ds(first, rows), :] = normed.astype(jnp.bfloat16)
+        for i, first in enumerate(firsts):
+            obuf[h, pl.ds(first, rows), :] = normed[i * rows : (i + 1) * rows].astype(jnp.bfloat16)
 
     def send_out(h, step):
         pair, _ = place(step)
@@ -217,22 +228,58 @@
                 device_id=(nxt, peer), device_id_type=MESH,
             ).start()
 
+    ahead = lax.rem(me_q, 2) == 1
+    behind = jnp.logical_not(ahead)
+    last_chip = lax.rem(me_q // 2, RUN) == RUN - 1
+
     forward_halo(0, 0)
     send_all(keys1)
     forward_halo(0, 1)
     send_all(values1)
     forward_halo(1, 0)
-    send_all(queries0)
+
+    @pl.when(ahead)
+    def _():
+        send_all(queries0)
+
     forward_halo(1, 1)
-    send_all(queries1)
+
+    @pl.when(behind)
+    def _():
+        pl.semaphore_wait(go_sem, 1)
+        send_all(queries0)
 
     for h in range(HEADS_DEV):
         wait_keys(h)
 
-        @pl.loop(0, ny)
+        if h == 0:
+
+            @pl.when(jnp.logical_and(ahead, jnp.logical_not(last_chip)))
+            def _():
+                pl.semaphore_signal(go_sem, inc=1, device_id=(prv, me), device_id_type=MESH)
+
+        @pl.loop(0, ny // 2)
         def _(step):
             attend(h, step)
-            send_out(h, step)
+            send_out(h, 2 * step)
+            send_out(h, 2 * step + 1)
+
+            if h + 1 < HEADS_DEV:
+                @pl.when(step == 0)
+                def _():
+                    send_first(*queries1)
+
+                @pl.when(step > 0)
+                def _():
+                    send_pair(*queries1, 2 * step)
+
+                send_pair(*queries1, 2 * step + 1)
+
+            if h == 0:
+
+                @pl.when(jnp.logical_and(jnp.logical_and(ahead, last_chip), step == 2))
+                def _():
+                    pl.semaphore_signal(go_sem, inc=1, device_id=(prv, me), device_id_type=MESH)
 
     for ref, sem in ((q_ref, q_send), (k_ref, k_send), (v_ref, v_send)):
         sent = ref.at[:, pl.ds(0, (ns - 1) * width)]
@@ -271,6 +318,7 @@
             dma, dma, dma,
             pltpu.SemaphoreType.REGULAR,
             pltpu.SemaphoreType.REGULAR,
+            pltpu.SemaphoreType.REGULAR,
         ],
         compiler_params=pltpu.CompilerParams(
             collective_id=0, has_side_effects=True, vmem_limit_bytes=56 * 2**20

time: 111 us -> 107 us (0.964)
  the two profiles are of different devices: /device:TPU:56 before, /device:TPU:387 now
where the time goes in v3:
time: 107 us
  Pallas kernels  104 us (97%)
  between operations  1.3 us (1%)
    pallas_call x1, Pallas kernels, per_device(): pl.pallas_call(functools.partial(kernel, nq, ns), out_shape=pltpu.VMEM((t...  104 us

profile of v3, /device:TPU:387, one launch (start us, length us, event | category | flops | bytes accessed | tf_op | source)
XLA Modules:
  0.0 106.8 jit_solution(1725012657245353196)
XLA Ops:
  1.3 104.5 %shard_map.64 = bf16[128,4096]{1,0:T(8,128)(2,1)S(1)} custom-call(bf16[128,4096]{1,0:T(8,128)(2,1)} %bitcast.5, bf16[128,4096]{1,0:T(8,128)(2,1)} %bitcast.6, bf16[128,4096]{1,0:T(8,128)(2,1)} %bitcast.7, f32[50,4096]{1,0:T(8,128)} %gains_ref.1, s32[1]{0:T(128)S(6)} %copy.9.level_ref, s32[1]{0:T(128)S(6)} %copy.10.halo_ref), custom_call_target="tpu_custom_call" | custom-call | flops 5368709120 | bytes 8388608 | tf_op jit(solution)/shard_map/pallas_call | solution.py:300
  105.8 1.0 copy.8

commit v4 on v3

--- a/solution.py
+++ b/solution.py
@@ -249,6 +249,12 @@
         pl.semaphore_wait(go_sem, 1)
         send_all(queries0)
 
+    at_once = jnp.logical_or(behind, last_chip)
+
+    @pl.when(at_once)
+    def _():
+        send_all(queries1)
+
     for h in range(HEADS_DEV):
         wait_keys(h)
 
@@ -265,15 +271,17 @@
             send_out(h, 2 * step + 1)
 
             if h + 1 < HEADS_DEV:
-                @pl.when(step == 0)
+                @pl.when(jnp.logical_not(at_once))
                 def _():
-                    send_first(*queries1)
-
-                @pl.when(step > 0)
-                def _():
-                    send_pair(*queries1, 2 * step)
-
-                send_pair(*queries1, 2 * step + 1)
+                    @pl.when(step == 0)
+                    def _():
+                        send_first(*queries1)
+
+                    @pl.when(step > 0)
+                    def _():
+                        send_pair(*queries1, 2 * step)
+
+                    send_pair(*queries1, 2 * step + 1)
 
             if h == 0:
 

time: 107 us -> 105 us (0.981)
  the two profiles are of different devices: /device:TPU:387 before, /device:TPU:23 now
where the time goes in v4:
time: 105 us
  Pallas kernels  103 us (98%)
  between operations  1.3 us (1%)
    pallas_call x1, Pallas kernels, per_device(): pl.pallas_call(functools.partial(kernel, nq, ns), out_shape=pltpu.VMEM((t...  103 us

profile of v4, /device:TPU:23, one launch (start us, length us, event | category | flops | bytes accessed | tf_op | source)
XLA Modules:
  0.0 104.9 jit_solution(7850681828859368835)
XLA Ops:
  1.3 102.6 %shard_map.64 = bf16[128,4096]{1,0:T(8,128)(2,1)S(1)} custom-call(bf16[128,4096]{1,0:T(8,128)(2,1)} %bitcast.5, bf16[128,4096]{1,0:T(8,128)(2,1)} %bitcast.6, bf16[128,4096]{1,0:T(8,128)(2,1)} %bitcast.7, f32[50,4096]{1,0:T(8,128)} %gains_ref.1, s32[1]{0:T(128)S(6)} %copy.9.level_ref, s32[1]{0:T(128)S(6)} %copy.10.halo_ref), custom_call_target="tpu_custom_call" | custom-call | flops 5368709120 | bytes 8388608 | tf_op jit(solution)/shard_map/pallas_call | solution.py:308
  103.9 1.0 copy.8

commit v5 on v3

--- a/solution.py
+++ b/solution.py
@@ -249,6 +249,8 @@
         pl.semaphore_wait(go_sem, 1)
         send_all(queries0)
 
+    send_all(queries1)
+
     for h in range(HEADS_DEV):
         wait_keys(h)
 
@@ -263,17 +265,6 @@
             attend(h, step)
             send_out(h, 2 * step)
             send_out(h, 2 * step + 1)
-
-            if h + 1 < HEADS_DEV:
-                @pl.when(step == 0)
-                def _():
-                    send_first(*queries1)
-
-                @pl.when(step > 0)
-                def _():
-                    send_pair(*queries1, 2 * step)
-
-                send_pair(*queries1, 2 * step + 1)
 
             if h == 0:
 

time: 107 us -> 105 us (0.981)
  the two profiles are of different devices: /device:TPU:387 before, /device:TPU:31 now
where the time goes in v5:
time: 105 us
  Pallas kernels  103 us (98%)
  between operations  1.3 us (1%)
    pallas_call x1, Pallas kernels, per_device(): pl.pallas_call(functools.partial(kernel, nq, ns), out_shape=pltpu.VMEM((t...  103 us

profile of v5, /device:TPU:31, one launch (start us, length us, event | category | flops | bytes accessed | tf_op | source)
XLA Modules:
  0.0 105.0 jit_solution(5754471928345768032)
XLA Ops:
  1.3 102.7 %shard_map.64 = bf16[128,4096]{1,0:T(8,128)(2,1)S(1)} custom-call(bf16[128,4096]{1,0:T(8,128)(2,1)} %bitcast.5, bf16[128,4096]{1,0:T(8,128)(2,1)} %bitcast.6, bf16[128,4096]{1,0:T(8,128)(2,1)} %bitcast.7, f32[50,4096]{1,0:T(8,128)} %gains_ref.1, s32[1]{0:T(128)S(6)} %copy.9.level_ref, s32[1]{0:T(128)S(6)} %copy.10.halo_ref), custom_call_target="tpu_custom_call" | custom-call | flops 5368709120 | bytes 8388608 | tf_op jit(solution)/shard_map/pallas_call | solution.py:291
  104.0 1.0 copy.8
